TPU v7x, 32 devices: a whole 2x2x4 slice. The times are simulated.
32 devices in a mesh: axial: 8 (over y, x, core), trans: 4 (over z).
Axes of the slice: x: 2, y: 2, z: 4, core: 2. Of those that a mesh axis runs over, the one named last changes fastest.
Arguments:
- concentration: float32 [128, 32, 256], P('axial', 'trans'), may hold values from -4 to 4
- pore_mask: int32 [128, 32, 256], P('axial', 'trans'), may hold values 0 or 1
- velocity: float32 [128, 32, 256], P('axial', 'trans'), may hold values from 20 to 80
Outputs:
- new_concentration: float32 [128, 32, 256], P('axial', 'trans')
All inputs are finite; a program needn't handle non-finite values. No bound on the sum of `pore_mask` on one device may be relied on, other than what follows from the above.
Results may differ from a plain program's by a relative error of at most 0.00028.
Values sent between devices are 32-bit elements; how exact they have to be, the bound alone decides.
A program may use at most 64 MiB of HBM per device.

v0:
```python
import jax
import jax.numpy as jnp
from jax import lax
from jax.sharding import PartitionSpec as P

axial_number = 800.0
trans_number = 0.5


def padded(cells, sides, width):
    for axis, dim in sides:
        count = lax.axis_size(axis)
        ends = count - 1
        head = lax.slice_in_dim(cells, 0, width, axis=dim)
        tail = lax.slice_in_dim(cells, cells.shape[dim] - width, cells.shape[dim], axis=dim)
        cells = jnp.concatenate(
            [
                lax.ppermute(tail, axis, [(i, (i + 1) % count) for i in range(ends)]),
                cells,
                lax.ppermute(head, axis, [((i + 1) % count, i) for i in range(ends)]),
            ],
            axis=dim,
        )
    return cells


def plane_term(field_pad, phi_pad, field_data, axis_dim):
    cells = field_data.shape[axis_dim]
    face_share = 0.5 * (
        lax.slice_in_dim(phi_pad, 0, cells + 1, axis=axis_dim)
        + lax.slice_in_dim(phi_pad, 1, cells + 2, axis=axis_dim)
    )
    upper_part = lax.slice_in_dim(face_share, 1, cells + 1, axis=axis_dim) * (
        lax.slice_in_dim(field_pad, 2, cells + 2, axis=axis_dim) - field_data
    )
    lower_part = lax.slice_in_dim(face_share, 0, cells, axis=axis_dim) * (
        lax.slice_in_dim(field_pad, 0, cells, axis=axis_dim) - field_data
    )
    return upper_part + lower_part


def eliminate(below_coef, main_coef, above_coef, rhs):
    cell_count = main_coef.shape[0]
    first_src = jnp.concatenate([-below_coef[1:2], jnp.zeros_like(main_coef[2 : cell_count - 1])])
    last_src = jnp.concatenate(
        [
            jnp.zeros_like(main_coef[1 : cell_count - 2]),
            -above_coef[cell_count - 2 : cell_count - 1],
        ]
    )
    sources = jnp.stack([first_src, last_src, rhs[1 : cell_count - 1]], axis=1)

    def forward(running, row_data):
        ratios, partials = running
        below_row, main_row, above_row, source_row = row_data
        pivot_value = main_row - below_row * ratios
        new_ratios = above_row / pivot_value
        new_partials = (source_row - below_row[None] * partials) / pivot_value[None]
        return ((new_ratios, new_partials), (new_ratios, new_partials))

    start_state = (jnp.zeros_like(main_coef[0]), jnp.zeros_like(sources[0]))
    inputs_inner = (
        below_coef[1 : cell_count - 1],
        main_coef[1 : cell_count - 1],
        above_coef[1 : cell_count - 1],
        sources,
    )
    _, (ratio_rows, partial_rows) = lax.scan(forward, start_state, inputs_inner)

    def backward(next_value, row_data):
        ratios, partials = row_data
        now_value = partials - ratios[None] * next_value
        return (now_value, now_value)

    _, interior = lax.scan(
        backward, jnp.zeros_like(partial_rows[0]), (ratio_rows, partial_rows), reverse=True
    )
    last_cell = cell_count - 1
    first_lower = below_coef[0]
    first_main = main_coef[0] + above_coef[0] * interior[0, 0]
    first_upper = above_coef[0] * interior[0, 1]
    first_rhs = rhs[0] - above_coef[0] * interior[0, 2]
    last_lower = below_coef[last_cell] * interior[-1, 0]
    last_main = main_coef[last_cell] + below_coef[last_cell] * interior[-1, 1]
    last_upper = above_coef[last_cell]
    last_rhs = rhs[last_cell] - below_coef[last_cell] * interior[-1, 2]
    reduced = jnp.stack(
        [
            jnp.stack([first_lower, last_lower]),
            jnp.stack([first_main, last_main]),
            jnp.stack([first_upper, last_upper]),
            jnp.stack([first_rhs, last_rhs]),
        ]
    )
    return (reduced, interior)


def assemble(first_cell, last_cell, interior):
    inner_cells = (
        interior[:, 0] * first_cell[None] + interior[:, 1] * last_cell[None] + interior[:, 2]
    )
    return jnp.concatenate([first_cell[None], inner_cells, last_cell[None]])


def reduce_cyclic(lower_part, main_part, upper_part, right_part):
    row_count = lower_part.shape[0]
    for stride_level in range(row_count.bit_length() - 1):
        stride = 2**stride_level

        def from_lower(values, fill_value):
            return jnp.concatenate(
                [jnp.full_like(values[:stride], fill_value), values[: row_count - stride]]
            )

        def from_upper(values, fill_value):
            return jnp.concatenate([values[stride:], jnp.full_like(values[:stride], fill_value)])

        factor_low = lower_part / from_lower(main_part, 1.0)
        factor_high = upper_part / from_upper(main_part, 1.0)
        new_lower = -factor_low * from_lower(lower_part, 0.0)
        new_main = (
            main_part
            - factor_low * from_lower(upper_part, 0.0)
            - factor_high * from_upper(lower_part, 0.0)
        )
        new_upper = -factor_high * from_upper(upper_part, 0.0)
        new_right = (
            right_part
            - factor_low * from_lower(right_part, 0.0)
            - factor_high * from_upper(right_part, 0.0)
        )
        lower_part, main_part, upper_part, right_part = (new_lower, new_main, new_upper, new_right)
    return right_part / main_part


def body(concentration, pore_mask, velocity):
    porosity = 0.1 + 0.9 * pore_mask.astype(jnp.float32)
    axial_ext = padded(jnp.stack([concentration, porosity, velocity]), (("axial", 1),), 1)
    conc_ext = axial_ext[0]
    phi_ext = axial_ext[1]
    vel_ext = axial_ext[2]
    face_share = 0.5 * (phi_ext[:-1] + phi_ext[1:])
    advect = 0.5 * (vel_ext[:-1] + vel_ext[1:]) * face_share
    spread = axial_number * face_share
    lower_coef = advect[:-1] + spread[:-1]
    upper_coef = spread[1:]
    center = spread[:-1] + spread[1:] + advect[1:]
    axial_term = lower_coef * conc_ext[:-2] - center * concentration + upper_coef * conc_ext[2:]
    plane_ext = padded(jnp.stack([concentration, porosity]), (("trans", 2),), 1)
    transverse = plane_term(plane_ext[0], plane_ext[1], concentration, 1)
    z_widths = ((0, 0), (0, 0), (1, 1))
    transverse = transverse + plane_term(
        jnp.pad(concentration, z_widths), jnp.pad(porosity, z_widths), concentration, 2
    )
    rhs = concentration + axial_term + trans_number * transverse
    below_coef = -lower_coef
    main_coef = 1.0 + center
    above_coef = -upper_coef
    device_index = lax.axis_index("axial")
    reduced, interior = eliminate(below_coef, main_coef, above_coef, rhs)
    gathered = lax.all_gather(reduced, "axial", axis=1, tiled=True)
    all_ends = reduce_cyclic(gathered[0], gathered[1], gathered[2], gathered[3])
    end_values = lax.dynamic_slice_in_dim(all_ends, 2 * device_index, 2, 0)
    return assemble(end_values[0], end_values[1], interior)


def solution(mesh):
    in_specs = (P("axial", "trans", None), P("axial", "trans", None), P("axial", "trans", None))
    out_specs = P("axial", "trans", None)
    return jax.shard_map(body, mesh=mesh, in_specs=in_specs, out_specs=out_specs, check_vma=False)
```

profile of v0, /device:TPU:0, one launch (start us, length us, event | category | flops | bytes accessed | tf_op | source)
XLA Modules:
  0.0 33.0 jit_solution(11848905922522627214)
XLA Ops:
  0.0 0.0 copy-start
  0.0 1.0 %fusion.47 = (f32[1,16,8,256]{3,2,1,0:T(8,128)S(1)}, f32[16,8,256]{2,1,0:T(8,128)S(1)}) fusion(s32[16,8,256]{2,1,0:T(8,128)} %param.8), kind=kLoop, calls=%fused_computation.145 | loop fusion | flops 98304 | bytes 393216 | tf_op jit(solution)/shard_map/stack | solution.py:138
  1.0 0.0 copy-done
  1.0 0.0 copy-done.1
  1.0 2.3 %collective-permute-start = (f32[3,1,8,256]{3,2,1,0:T(8,128)S(1)}, f32[3,1,8,256]{3,2,1,0:T(8,128)S(1)}, u32[]{:S(2)}, u32[]{:S(2)}) collective-permute-start(f32[3,1,8,256]{3,2,1,0:T(8,128)S(1)} %get-tuple-element.278), channel_id=1, source_target_pairs={{0,4},{4,8},{8,12},{12,16},{16,20},{20,24},{24,28},{1,5},{5,9},{9,... | collective-permute-start | bytes 73736 | tf_op jit(solution)/shard_map/ppermute | solution.py:18
  3.4 1.3 %collective-permute-start.1 = (f32[3,1,8,256]{3,2,1,0:T(8,128)S(1)}, f32[3,1,8,256]{3,2,1,0:T(8,128)S(1)}, u32[]{:S(2)}, u32[]{:S(2)}) collective-permute-start(f32[3,1,8,256]{3,2,1,0:T(8,128)S(1)} %get-tuple-element.279), channel_id=1, source_target_pairs={{4,0},{8,4},{12,8},{16,12},{20,16},{24,20},{28,24},{5,1},{9,5},{13... | collective-permute-start | bytes 73736 | tf_op jit(solution)/shard_map/ppermute | solution.py:20
  4.7 4.3 %collective-permute-start.2 = (f32[2,16,1,256]{3,2,1,0:T(1,128)S(1)}, f32[2,16,1,256]{3,2,1,0:T(1,128)S(1)}, u32[]{:S(2)}, u32[]{:S(2)}) collective-permute-start(f32[2,16,1,256]{3,2,1,0:T(1,128)S(1)} %get-tuple-element.282), channel_id=1, source_target_pairs={{0,1},{1,2},{2,3},{4,5},{5,6},{6,7},{8,9},{9,10},{10,11},{12,13},{... | collective-permute-start | bytes 98312 | tf_op jit(solution)/shard_map/ppermute | solution.py:18
  9.1 1.3 %collective-permute-start.3 = (f32[2,16,1,256]{3,2,1,0:T(1,128)S(1)}, f32[2,16,1,256]{3,2,1,0:T(1,128)S(1)}, u32[]{:S(2)}, u32[]{:S(2)}) collective-permute-start(f32[2,16,1,256]{3,2,1,0:T(1,128)S(1)} %get-tuple-element.283), channel_id=1, source_target_pairs={{1,0},{2,1},{3,2},{5,4},{6,5},{7,6},{9,8},{10,9},{11,10},{13,12},{... | collective-permute-start | bytes 98312 | tf_op jit(solution)/shard_map/ppermute | solution.py:20
  10.4 0.1 fusion.3
  10.5 0.0 collective-permute-done
  10.5 0.0 collective-permute-done.1
  10.5 0.1 maximum_maximum_fusion
  10.8 0.0 copy-start.2
  10.8 0.6 %copy-done.2 = f32[16,8,256]{2,1,0:T(8,128)} copy-done((f32[16,8,256]{2,1,0:T(8,128)}, f32[16,8,256]{2,1,0:T(8,128)S(1)}, u32[]{:S(2)}) %copy-start.2) | copy-done | bytes 131096
  11.4 0.0 collective-permute-done.2
  11.4 3.4 %collective-permute-done.3 = f32[2,16,1,256]{3,2,1,0:T(1,128)S(1)} collective-permute-done((f32[2,16,1,256]{3,2,1,0:T(1,128)S(1)}, f32[2,16,1,256]{3,2,1,0:T(1,128)S(1)}, u32[]{:S(2)}, u32[]{:S(2)}) %collective-permute-start.3) | collective-permute-done | bytes 32800 | tf_op jit(solution)/shard_map/ppermute | solution.py:20
  14.9 0.1 pad_maximum_fusion
  15.1 0.2 fusion.11
  15.3 0.0 slice-start
  15.4 0.9 %slice-done = f32[14,8,256]{2,1,0:T(8,128)S(1)} async-done(((f32[16,8,256]{2,1,0:T(8,128)}), f32[14,8,256]{2,1,0:T(8,128)S(1)}, s32[]{:S(2)}) %slice-start) | async-done | bytes 114712 | tf_op jit(solution)/shard_map/slice | solution.py:64
  16.2 0.9 %while.34 = (s32[]{:T(128)}, f32[8,256]{1,0:T(8,128)S(1)}, f32[3,8,256]{2,1,0:T(8,128)S(1)}, f32[14,8,256]{2,1,0:T(8,128)S(1)}, f32[14,3,8,256]{3,2,1,0:T(8,128)...) while((s32[]{:T(128)}, f32[8,256]{1,0:T(8,128)S(1)}, ...), condition=%wide.region_1.2_spmd.clone, body=%wide.region_0.1_spmd.clone.sunk | while | flops 32771 | bytes 180352 | solution.py:68
  17.1 0.0 copy-start.3
  17.1 0.8 %while.35 = (s32[]{:T(128)}, f32[3,8,256]{2,1,0:T(8,128)S(1)}, f32[14,3,8,256]{3,2,1,0:T(8,128)S(1)}, f32[14,3,8,256]{3,2,1,0:T(8,128)S(1)}, f32[14,8,256]{2,1,0...) while((s32[]{:T(128)}, f32[3,8,256]{2,1,0:T(8,128)S(1)}, f32[14,3,8,256]{3,2,1,0:T(8,128)S(1)}, ...), condition=%wide.region_3.4_spmd.clone, body=%wide.region_2.3_spmd.clone.sunk | while | flops 18436 | bytes 122995 | solution.py:75
  18.0 0.1 copy-done.3
  18.1 13.3 %all_gather.3 = f32[4,16,8,256]{3,2,1,0:T(8,128)S(1)} all-gather(f32[4,2,8,256]{3,2,1,0:T(8,128)S(1)} %pad_maximum_fusion.4), channel_id=1, replica_groups=mesh['axial'=8,'trans'=4] {'axial'}, dimensions={1}, use_global_device_ids=true | all-gather | bytes 589824 | tf_op jit(solution)/shard_map/all_gather | solution.py:161
  31.4 0.1 slice_bitcast_fusion.9
  31.5 0.1 fusion.15
  31.6 0.1 multiply_subtract_fusion.3
  31.8 0.1 multiply_subtract_fusion.2
  31.9 0.1 multiply_subtract_fusion.1
  32.1 0.1 pad_multiply_fusion.1
  32.3 0.7 %pad_maximum_fusion.3 = f32[16,8,256]{2,1,0:T(8,128)} fusion(f32[1,8,256]{2,1,0:T(8,128)S(1)} %get-tuple-element.316, f32[14,8,256]{2,1,0:T(8,128)S(1)} %fusion.29, f32[1,8,256]{2,1,0:T(8,128)S(1)} %get-tuple-element.313), kind=kLoop, calls=%fused_computation.64 | loop fusion | flops 65536 | bytes 262144 | tf_op jit(solution)/shard_map/concatenate | solution.py:102
  (98 shorter events, 1.4 us)
Async XLA Ops:
  0.0 1.0 %copy-start = (f32[16,8,256]{2,1,0:T(8,128)S(1)}, f32[16,8,256]{2,1,0:T(8,128)}, u32[]{:S(2)}) copy-start(f32[16,8,256]{2,1,0:T(8,128)} %param.7) | copy-start | bytes 393220
  0.0 1.0 %copy-start.1 = (f32[16,8,256]{2,1,0:T(8,128)S(1)}, f32[16,8,256]{2,1,0:T(8,128)}, u32[]{:S(2)}) copy-start(f32[16,8,256]{2,1,0:T(8,128)} %param.9) | copy-start | bytes 393220
  1.0 9.5 %collective-permute-start = (f32[3,1,8,256]{3,2,1,0:T(8,128)S(1)}, f32[3,1,8,256]{3,2,1,0:T(8,128)S(1)}, u32[]{:S(2)}, u32[]{:S(2)}) collective-permute-start(f32[3,1,8,256]{3,2,1,0:T(8,128)S(1)} %get-tuple-element.278), channel_id=1, source_target_pairs={{0,4},{4,8},{8,12},{12,16},{16,20},{20,24},{24,28},{1,5},{5,9},{9,... | collective-permute-start | bytes 73736 | tf_op jit(solution)/shard_map/ppermute | solution.py:18
  3.4 7.1 %collective-permute-start.1 = (f32[3,1,8,256]{3,2,1,0:T(8,128)S(1)}, f32[3,1,8,256]{3,2,1,0:T(8,128)S(1)}, u32[]{:S(2)}, u32[]{:S(2)}) collective-permute-start(f32[3,1,8,256]{3,2,1,0:T(8,128)S(1)} %get-tuple-element.279), channel_id=1, source_target_pairs={{4,0},{8,4},{12,8},{16,12},{20,16},{24,20},{28,24},{5,1},{9,5},{13... | collective-permute-start | bytes 73736 | tf_op jit(solution)/shard_map/ppermute | solution.py:20
  4.7 6.7 %collective-permute-start.2 = (f32[2,16,1,256]{3,2,1,0:T(1,128)S(1)}, f32[2,16,1,256]{3,2,1,0:T(1,128)S(1)}, u32[]{:S(2)}, u32[]{:S(2)}) collective-permute-start(f32[2,16,1,256]{3,2,1,0:T(1,128)S(1)} %get-tuple-element.282), channel_id=1, source_target_pairs={{0,1},{1,2},{2,3},{4,5},{5,6},{6,7},{8,9},{9,10},{10,11},{12,13},{... | collective-permute-start | bytes 98312 | tf_op jit(solution)/shard_map/ppermute | solution.py:18
  9.1 5.8 %collective-permute-start.3 = (f32[2,16,1,256]{3,2,1,0:T(1,128)S(1)}, f32[2,16,1,256]{3,2,1,0:T(1,128)S(1)}, u32[]{:S(2)}, u32[]{:S(2)}) collective-permute-start(f32[2,16,1,256]{3,2,1,0:T(1,128)S(1)} %get-tuple-element.283), channel_id=1, source_target_pairs={{1,0},{2,1},{3,2},{5,4},{6,5},{7,6},{9,8},{10,9},{11,10},{13,12},{... | collective-permute-start | bytes 98312 | tf_op jit(solution)/shard_map/ppermute | solution.py:20
  10.8 0.7 %copy-start.2 = (f32[16,8,256]{2,1,0:T(8,128)}, f32[16,8,256]{2,1,0:T(8,128)S(1)}, u32[]{:S(2)}) copy-start(f32[16,8,256]{2,1,0:T(8,128)S(1)} %broadcast_add_fusion) | copy-start | bytes 393220
  15.3 0.9 %slice-start = ((f32[16,8,256]{2,1,0:T(8,128)}), f32[14,8,256]{2,1,0:T(8,128)S(1)}, s32[]{:S(2)}) async-start(f32[16,8,256]{2,1,0:T(8,128)} %copy-done.2), calls=%async_computation | async-start | bytes 229376 | tf_op jit(solution)/shard_map/slice | solution.py:64
  17.1 0.9 %copy-start.3 = (f32[16,8,256]{2,1,0:T(8,128)S(1)}, f32[16,8,256]{2,1,0:T(8,128)}, u32[]{:S(2)}) copy-start(f32[16,8,256]{2,1,0:T(8,128)} %copy-done.2) | copy-start | bytes 393220
where the time goes:
time: 33.2 us; the launch traced here: 33 us
  blocking collectives  13.3 us (40%)
  starting transfers between devices  9.24 us (28%)
  other arithmetic  3.51 us (11%)
  waiting for transfers between devices  3.45 us (10%)
  local copies, waits for them, and re-layouts  2.09 us (6%)
  loops' own time  0.93 us (3%)
  between operations  0.44 us (1%)
    all_gather x1, blocking collectives, body(): gathered = lax.all_gather(reduced, 'axial', axis=1, tiled=True)  13.3 us
    ppermute x2, starting transfers between devices, padded(): lax.ppermute(tail, axis, [(i, (i + 1) % count) for i in range(ends)])  6.66 us
    ppermute x2, waiting for transfers between devices, padded(): lax.ppermute(head, axis, [((i + 1) % count, i) for i in range(ends)])  3.45 us
    ppermute x2, starting transfers between devices, padded(): lax.ppermute(head, axis, [((i + 1) % count, i) for i in range(ends)])  2.58 us
    another operation x1, other arithmetic, body(): jnp.stack([concentration, porosity, velocity])  0.97 us
    slice x2, local copies, waits for them, and re-layouts, eliminate(): main_coef[1:cell_count - 1]  0.86 us
    unnamed x8, local copies, waits for them, and re-layouts  0.75 us
    concatenate x1, other arithmetic, assemble(): return jnp.concatenate([first_cell[None], inner_cells, last_cell[None]])  0.67 us
  transfers between devices with their start and end apart: 4, of which 1 were waited for; matrix products, arithmetic and copies ran while one was open for 1% of the time, Pallas kernels for 0%

commit v1 on v0

--- a/solution.py
+++ b/solution.py
@@ -158,7 +158,25 @@
     above_coef = -upper_coef
     device_index = lax.axis_index("axial")
     reduced, interior = eliminate(below_coef, main_coef, above_coef, rhs)
-    gathered = lax.all_gather(reduced, "axial", axis=1, tiled=True)
+    low, odd, everything = (lax.axis_size("axial"), lax.axis_index("axial"), reduced.shape[1])
+    buffers = tuple(((to_i, (to_i + 1) % low) for to_i in range(low)))
+    stack_in = tuple(((to_i, (to_i - 1) % low) for to_i in range(low)))
+    gathered = jnp.zeros(
+        (*reduced.shape[:1], low * everything, *reduced.shape[1 + 1 :]), reduced.dtype
+    )
+    gathered = lax.dynamic_update_slice_in_dim(gathered, reduced, odd * everything, axis=1)
+    w2 = work_now = reduced
+    step_out = low // 2
+    for dev_j in range(1, step_out + 1):
+        w2 = lax.ppermute(w2, axis_name="axial", perm=buffers)
+        gathered = lax.dynamic_update_slice_in_dim(
+            gathered, w2, (odd - dev_j) % low * everything, axis=1
+        )
+        if dev_j < low - step_out:
+            work_now = lax.ppermute(work_now, perm=stack_in, axis_name="axial")
+            gathered = lax.dynamic_update_slice_in_dim(
+                gathered, work_now, (odd + dev_j) % low * everything, axis=1
+            )
     all_ends = reduce_cyclic(gathered[0], gathered[1], gathered[2], gathered[3])
     end_values = lax.dynamic_slice_in_dim(all_ends, 2 * device_index, 2, 0)
     return assemble(end_values[0], end_values[1], interior)

time: 33.2 us -> 41 us (1.23)
  the two profiles are of different devices: /device:TPU:0 before, /device:TPU:20 now
where the time goes in v1:
time: 41 us; the launch traced here: 40.8 us
  starting transfers between devices  20.4 us (50%)
  waiting for transfers between devices  13.2 us (32%)
  other arithmetic  3.51 us (9%)
  local copies, waits for them, and re-layouts  2.19 us (5%)
  loops' own time  0.93 us (2%)
  between operations  0.5 us (1%)
    ppermute x4, waiting for transfers between devices, body(): w2 = lax.ppermute(w2, axis_name='axial', perm=buffers)  10.6 us
    ppermute x3, starting transfers between devices, body(): work_now = lax.ppermute(work_now, perm=stack_in, axis_name='axial')  8.08 us
    ppermute x2, starting transfers between devices, padded(): lax.ppermute(head, axis, [((i + 1) % count, i) for i in range(ends)])  6.9 us
    ppermute x2, starting transfers between devices, padded(): lax.ppermute(tail, axis, [(i, (i + 1) % count) for i in range(ends)])  5.39 us
    ppermute x2, waiting for transfers between devices, padded(): lax.ppermute(head, axis, [((i + 1) % count, i) for i in range(ends)])  2.38 us
    another operation x1, other arithmetic, body(): jnp.stack([concentration, porosity, velocity])  0.97 us
    slice x2, local copies, waits for them, and re-layouts, eliminate(): main_coef[1:cell_count - 1]  0.86 us
  transfers between devices with their start and end apart: 11, of which 6 were waited for; matrix products, arithmetic and copies ran while one was open for 1% of the time, Pallas kernels for 0%

profile of v1, /device:TPU:20, one launch (start us, length us, event | category | flops | bytes accessed | tf_op | source)
XLA Modules:
  0.0 40.8 jit_solution(16910277212396187911)
XLA Ops:
  0.0 1.0 %fusion.47 = (f32[1,16,8,256]{3,2,1,0:T(8,128)S(1)}, f32[16,8,256]{2,1,0:T(8,128)S(1)}) fusion(s32[16,8,256]{2,1,0:T(8,128)} %param.8), kind=kLoop, calls=%fused_computation.153 | loop fusion | flops 98304 | bytes 393216 | tf_op jit(solution)/shard_map/stack | solution.py:138
  1.0 0.0 copy-done.1
  1.0 1.9 %collective-permute-start = (f32[3,1,8,256]{3,2,1,0:T(8,128)S(1)}, f32[3,1,8,256]{3,2,1,0:T(8,128)S(1)}, u32[]{:S(2)}, u32[]{:S(2)}) collective-permute-start(f32[3,1,8,256]{3,2,1,0:T(8,128)S(1)} %get-tuple-element.278), channel_id=1, source_target_pairs={{0,4},{4,8},{8,12},{12,16},{16,20},{20,24},{24,28},{1,5},{5,9},{9,... | collective-permute-start | bytes 73736 | tf_op jit(solution)/shard_map/ppermute | solution.py:18
  3.0 4.5 %collective-permute-start.1 = (f32[3,1,8,256]{3,2,1,0:T(8,128)S(1)}, f32[3,1,8,256]{3,2,1,0:T(8,128)S(1)}, u32[]{:S(2)}, u32[]{:S(2)}) collective-permute-start(f32[3,1,8,256]{3,2,1,0:T(8,128)S(1)} %get-tuple-element.279), channel_id=1, source_target_pairs={{4,0},{8,4},{12,8},{16,12},{20,16},{24,20},{28,24},{5,1},{9,5},{13... | collective-permute-start | bytes 73736 | tf_op jit(solution)/shard_map/ppermute | solution.py:20
  7.6 3.5 %collective-permute-start.2 = (f32[2,16,1,256]{3,2,1,0:T(1,128)S(1)}, f32[2,16,1,256]{3,2,1,0:T(1,128)S(1)}, u32[]{:S(2)}, u32[]{:S(2)}) collective-permute-start(f32[2,16,1,256]{3,2,1,0:T(1,128)S(1)} %get-tuple-element.282), channel_id=1, source_target_pairs={{0,1},{1,2},{2,3},{4,5},{5,6},{6,7},{8,9},{9,10},{10,11},{12,13},{... | collective-permute-start | bytes 98312 | tf_op jit(solution)/shard_map/ppermute | solution.py:18
  11.0 2.4 %collective-permute-start.3 = (f32[2,16,1,256]{3,2,1,0:T(1,128)S(1)}, f32[2,16,1,256]{3,2,1,0:T(1,128)S(1)}, u32[]{:S(2)}, u32[]{:S(2)}) collective-permute-start(f32[2,16,1,256]{3,2,1,0:T(1,128)S(1)} %get-tuple-element.283), channel_id=1, source_target_pairs={{1,0},{2,1},{3,2},{5,4},{6,5},{7,6},{9,8},{10,9},{11,10},{13,12},{... | collective-permute-start | bytes 98312 | tf_op jit(solution)/shard_map/ppermute | solution.py:20
  13.4 0.1 fusion.3
  13.6 0.1 maximum_maximum_fusion
  13.9 0.6 %copy-done.2 = f32[16,8,256]{2,1,0:T(8,128)} copy-done((f32[16,8,256]{2,1,0:T(8,128)}, f32[16,8,256]{2,1,0:T(8,128)S(1)}, u32[]{:S(2)}) %copy-start.2) | copy-done | bytes 131096
  14.5 2.4 %collective-permute-done.3 = f32[2,16,1,256]{3,2,1,0:T(1,128)S(1)} collective-permute-done((f32[2,16,1,256]{3,2,1,0:T(1,128)S(1)}, f32[2,16,1,256]{3,2,1,0:T(1,128)S(1)}, u32[]{:S(2)}, u32[]{:S(2)}) %collective-permute-start.3) | collective-permute-done | bytes 32800 | tf_op jit(solution)/shard_map/ppermute | solution.py:20
  16.9 0.1 pad_maximum_fusion
  17.0 0.2 fusion.11
  17.3 0.9 %slice-done = f32[14,8,256]{2,1,0:T(8,128)S(1)} async-done(((f32[16,8,256]{2,1,0:T(8,128)}), f32[14,8,256]{2,1,0:T(8,128)S(1)}, s32[]{:S(2)}) %slice-start) | async-done | bytes 114712 | tf_op jit(solution)/shard_map/slice | solution.py:64
  18.2 0.9 %while.34 = (s32[]{:T(128)}, f32[8,256]{1,0:T(8,128)S(1)}, f32[3,8,256]{2,1,0:T(8,128)S(1)}, f32[14,8,256]{2,1,0:T(8,128)S(1)}, f32[14,3,8,256]{3,2,1,0:T(8,128)...) while((s32[]{:T(128)}, f32[8,256]{1,0:T(8,128)S(1)}, ...), condition=%wide.region_1.2_spmd.clone, body=%wide.region_0.1_spmd.clone.sunk | while | flops 32771 | bytes 180352 | solution.py:68
  19.1 0.8 %while.35 = (s32[]{:T(128)}, f32[3,8,256]{2,1,0:T(8,128)S(1)}, f32[14,3,8,256]{3,2,1,0:T(8,128)S(1)}, f32[14,3,8,256]{3,2,1,0:T(8,128)S(1)}, f32[14,8,256]{2,1,0...) while((s32[]{:T(128)}, f32[3,8,256]{2,1,0:T(8,128)S(1)}, f32[14,3,8,256]{3,2,1,0:T(8,128)S(1)}, ...), condition=%wide.region_3.4_spmd.clone, body=%wide.region_2.3_spmd.clone.sunk | while | flops 18436 | bytes 122995 | solution.py:75
  19.9 0.1 copy-done.3
  20.1 0.1 collective-permute-start.4
  20.2 2.6 %collective-permute-start.5 = (f32[4,2,8,256]{3,2,1,0:T(8,128)S(1)}, f32[4,2,8,256]{3,2,1,0:T(8,128)S(1)}, u32[]{:S(2)}, u32[]{:S(2)}) collective-permute-start(f32[4,2,8,256]{3,2,1,0:T(8,128)S(1)} %get-tuple-element.313), channel_id=1, source_target_pairs={{0,28},{4,0},{8,4},{12,8},{16,12},{20,16},{24,20},{28,24},{1,29},{... | collective-permute-start | bytes 196616 | tf_op jit(solution)/shard_map/ppermute | solution.py:176
  22.8 2.6 %collective-permute-done.4 = f32[4,2,8,256]{3,2,1,0:T(8,128)S(1)} collective-permute-done((f32[4,2,8,256]{3,2,1,0:T(8,128)S(1)}, f32[4,2,8,256]{3,2,1,0:T(8,128)S(1)}, u32[]{:S(2)}, u32[]{:S(2)}) %collective-permute-start.4) | collective-permute-done | bytes 65568 | tf_op jit(solution)/shard_map/ppermute | solution.py:171
  25.4 2.6 %collective-permute-start.7 = (f32[4,2,8,256]{3,2,1,0:T(8,128)S(1)}, f32[4,2,8,256]{3,2,1,0:T(8,128)S(1)}, u32[]{:S(2)}, u32[]{:S(2)}) collective-permute-start(f32[4,2,8,256]{3,2,1,0:T(8,128)S(1)} %collective-permute-done.5), channel_id=1, source_target_pairs={{0,28},{4,0},{8,4},{12,8},{16,12},{20,16},{24,20},{28,24},{1,29},{... | collective-permute-start | bytes 196616 | tf_op jit(solution)/shard_map/ppermute | solution.py:176
  28.1 1.9 %collective-permute-done.6 = f32[4,2,8,256]{3,2,1,0:T(8,128)S(1)} collective-permute-done((f32[4,2,8,256]{3,2,1,0:T(8,128)S(1)}, f32[4,2,8,256]{3,2,1,0:T(8,128)S(1)}, u32[]{:S(2)}, u32[]{:S(2)}) %collective-permute-start.6) | collective-permute-done | bytes 65568 | tf_op jit(solution)/shard_map/ppermute | solution.py:171
  30.1 2.8 %collective-permute-start.9 = (f32[4,2,8,256]{3,2,1,0:T(8,128)S(1)}, f32[4,2,8,256]{3,2,1,0:T(8,128)S(1)}, u32[]{:S(2)}, u32[]{:S(2)}) collective-permute-start(f32[4,2,8,256]{3,2,1,0:T(8,128)S(1)} %collective-permute-done.7), channel_id=1, source_target_pairs={{0,28},{4,0},{8,4},{12,8},{16,12},{20,16},{24,20},{28,24},{1,29},{... | collective-permute-start | bytes 196616 | tf_op jit(solution)/shard_map/ppermute | solution.py:176
  32.9 1.7 %collective-permute-done.8 = f32[4,2,8,256]{3,2,1,0:T(8,128)S(1)} collective-permute-done((f32[4,2,8,256]{3,2,1,0:T(8,128)S(1)}, f32[4,2,8,256]{3,2,1,0:T(8,128)S(1)}, u32[]{:S(2)}, u32[]{:S(2)}) %collective-permute-start.8) | collective-permute-done | bytes 65568 | tf_op jit(solution)/shard_map/ppermute | solution.py:171
  34.6 0.2 collective-permute-done.9
  34.8 4.4 %collective-permute-done.10 = f32[4,2,8,256]{3,2,1,0:T(8,128)S(1)} collective-permute-done((f32[4,2,8,256]{3,2,1,0:T(8,128)S(1)}, f32[4,2,8,256]{3,2,1,0:T(8,128)S(1)}, u32[]{:S(2)}, u32[]{:S(2)}) %collective-permute-start.10) | collective-permute-done | bytes 65568 | tf_op jit(solution)/shard_map/ppermute | solution.py:171
  39.2 0.1 slice_bitcast_fusion.9
  39.3 0.1 fusion.15
  39.5 0.1 multiply_subtract_fusion.3
  39.6 0.1 multiply_subtract_fusion.2
  39.7 0.1 multiply_subtract_fusion.1
  39.9 0.1 pad_multiply_fusion.1
  40.1 0.7 %pad_maximum_fusion.3 = f32[16,8,256]{2,1,0:T(8,128)} fusion(f32[1,8,256]{2,1,0:T(8,128)S(1)} %get-tuple-element.318, f32[14,8,256]{2,1,0:T(8,128)S(1)} %fusion.29, f32[1,8,256]{2,1,0:T(8,128)S(1)} %get-tuple-element.315), kind=kLoop, calls=%fused_computation.64 | loop fusion | flops 65536 | bytes 262144 | tf_op jit(solution)/shard_map/concatenate | solution.py:102
  (119 shorter events, 1.6 us)
Async XLA Ops:
  0.0 1.0 %copy-start = (f32[16,8,256]{2,1,0:T(8,128)S(1)}, f32[16,8,256]{2,1,0:T(8,128)}, u32[]{:S(2)}) copy-start(f32[16,8,256]{2,1,0:T(8,128)} %param.7) | copy-start | bytes 393220
  0.0 1.0 %copy-start.1 = (f32[16,8,256]{2,1,0:T(8,128)S(1)}, f32[16,8,256]{2,1,0:T(8,128)}, u32[]{:S(2)}) copy-start(f32[16,8,256]{2,1,0:T(8,128)} %param.9) | copy-start | bytes 393220
  1.0 12.5 %collective-permute-start = (f32[3,1,8,256]{3,2,1,0:T(8,128)S(1)}, f32[3,1,8,256]{3,2,1,0:T(8,128)S(1)}, u32[]{:S(2)}, u32[]{:S(2)}) collective-permute-start(f32[3,1,8,256]{3,2,1,0:T(8,128)S(1)} %get-tuple-element.278), channel_id=1, source_target_pairs={{0,4},{4,8},{8,12},{12,16},{16,20},{20,24},{24,28},{1,5},{5,9},{9,... | collective-permute-start | bytes 73736 | tf_op jit(solution)/shard_map/ppermute | solution.py:18
  3.0 10.6 %collective-permute-start.1 = (f32[3,1,8,256]{3,2,1,0:T(8,128)S(1)}, f32[3,1,8,256]{3,2,1,0:T(8,128)S(1)}, u32[]{:S(2)}, u32[]{:S(2)}) collective-permute-start(f32[3,1,8,256]{3,2,1,0:T(8,128)S(1)} %get-tuple-element.279), channel_id=1, source_target_pairs={{4,0},{8,4},{12,8},{16,12},{20,16},{24,20},{28,24},{5,1},{9,5},{13... | collective-permute-start | bytes 73736 | tf_op jit(solution)/shard_map/ppermute | solution.py:20
  7.6 6.9 %collective-permute-start.2 = (f32[2,16,1,256]{3,2,1,0:T(1,128)S(1)}, f32[2,16,1,256]{3,2,1,0:T(1,128)S(1)}, u32[]{:S(2)}, u32[]{:S(2)}) collective-permute-start(f32[2,16,1,256]{3,2,1,0:T(1,128)S(1)} %get-tuple-element.282), channel_id=1, source_target_pairs={{0,1},{1,2},{2,3},{4,5},{5,6},{6,7},{8,9},{9,10},{10,11},{12,13},{... | collective-permute-start | bytes 98312 | tf_op jit(solution)/shard_map/ppermute | solution.py:18
  11.0 5.8 %collective-permute-start.3 = (f32[2,16,1,256]{3,2,1,0:T(1,128)S(1)}, f32[2,16,1,256]{3,2,1,0:T(1,128)S(1)}, u32[]{:S(2)}, u32[]{:S(2)}) collective-permute-start(f32[2,16,1,256]{3,2,1,0:T(1,128)S(1)} %get-tuple-element.283), channel_id=1, source_target_pairs={{1,0},{2,1},{3,2},{5,4},{6,5},{7,6},{9,8},{10,9},{11,10},{13,12},{... | collective-permute-start | bytes 98312 | tf_op jit(solution)/shard_map/ppermute | solution.py:20
  13.8 0.7 %copy-start.2 = (f32[16,8,256]{2,1,0:T(8,128)}, f32[16,8,256]{2,1,0:T(8,128)S(1)}, u32[]{:S(2)}) copy-start(f32[16,8,256]{2,1,0:T(8,128)S(1)} %broadcast_add_fusion) | copy-start | bytes 393220
  17.3 0.9 %slice-start = ((f32[16,8,256]{2,1,0:T(8,128)}), f32[14,8,256]{2,1,0:T(8,128)S(1)}, s32[]{:S(2)}) async-start(f32[16,8,256]{2,1,0:T(8,128)} %copy-done.2), calls=%async_computation | async-start | bytes 229376 | tf_op jit(solution)/shard_map/slice | solution.py:64
  19.1 0.9 %copy-start.3 = (f32[16,8,256]{2,1,0:T(8,128)S(1)}, f32[16,8,256]{2,1,0:T(8,128)}, u32[]{:S(2)}) copy-start(f32[16,8,256]{2,1,0:T(8,128)} %copy-done.2) | copy-start | bytes 393220
  20.1 5.3 %collective-permute-start.4 = (f32[4,2,8,256]{3,2,1,0:T(8,128)S(1)}, f32[4,2,8,256]{3,2,1,0:T(8,128)S(1)}, u32[]{:S(2)}, u32[]{:S(2)}) collective-permute-start(f32[4,2,8,256]{3,2,1,0:T(8,128)S(1)} %get-tuple-element.313), channel_id=1, source_target_pairs={{0,4},{4,8},{8,12},{12,16},{16,20},{20,24},{24,28},{28,0},{1,5},{5... | collective-permute-start | bytes 196616 | tf_op jit(solution)/shard_map/ppermute | solution.py:171
  20.2 5.2 %collective-permute-start.5 = (f32[4,2,8,256]{3,2,1,0:T(8,128)S(1)}, f32[4,2,8,256]{3,2,1,0:T(8,128)S(1)}, u32[]{:S(2)}, u32[]{:S(2)}) collective-permute-start(f32[4,2,8,256]{3,2,1,0:T(8,128)S(1)} %get-tuple-element.313), channel_id=1, source_target_pairs={{0,28},{4,0},{8,4},{12,8},{16,12},{20,16},{24,20},{28,24},{1,29},{... | collective-permute-start | bytes 196616 | tf_op jit(solution)/shard_map/ppermute | solution.py:176
  25.4 4.6 %collective-permute-start.6 = (f32[4,2,8,256]{3,2,1,0:T(8,128)S(1)}, f32[4,2,8,256]{3,2,1,0:T(8,128)S(1)}, u32[]{:S(2)}, u32[]{:S(2)}) collective-permute-start(f32[4,2,8,256]{3,2,1,0:T(8,128)S(1)} %collective-permute-done.4), channel_id=1, source_target_pairs={{0,4},{4,8},{8,12},{12,16},{16,20},{20,24},{24,28},{28,0},{1,5},{5... | collective-permute-start | bytes 196616 | tf_op jit(solution)/shard_map/ppermute | solution.py:171
  25.4 4.7 %collective-permute-start.7 = (f32[4,2,8,256]{3,2,1,0:T(8,128)S(1)}, f32[4,2,8,256]{3,2,1,0:T(8,128)S(1)}, u32[]{:S(2)}, u32[]{:S(2)}) collective-permute-start(f32[4,2,8,256]{3,2,1,0:T(8,128)S(1)} %collective-permute-done.5), channel_id=1, source_target_pairs={{0,28},{4,0},{8,4},{12,8},{16,12},{20,16},{24,20},{28,24},{1,29},{... | collective-permute-start | bytes 196616 | tf_op jit(solution)/shard_map/ppermute | solution.py:176
  30.0 4.6 %collective-permute-start.8 = (f32[4,2,8,256]{3,2,1,0:T(8,128)S(1)}, f32[4,2,8,256]{3,2,1,0:T(8,128)S(1)}, u32[]{:S(2)}, u32[]{:S(2)}) collective-permute-start(f32[4,2,8,256]{3,2,1,0:T(8,128)S(1)} %collective-permute-done.6), channel_id=1, source_target_pairs={{0,4},{4,8},{8,12},{12,16},{16,20},{20,24},{24,28},{28,0},{1,5},{5... | collective-permute-start | bytes 196616 | tf_op jit(solution)/shard_map/ppermute | solution.py:171
  30.1 4.7 %collective-permute-start.9 = (f32[4,2,8,256]{3,2,1,0:T(8,128)S(1)}, f32[4,2,8,256]{3,2,1,0:T(8,128)S(1)}, u32[]{:S(2)}, u32[]{:S(2)}) collective-permute-start(f32[4,2,8,256]{3,2,1,0:T(8,128)S(1)} %collective-permute-done.7), channel_id=1, source_target_pairs={{0,28},{4,0},{8,4},{12,8},{16,12},{20,16},{24,20},{28,24},{1,29},{... | collective-permute-start | bytes 196616 | tf_op jit(solution)/shard_map/ppermute | solution.py:176
  34.6 4.6 %collective-permute-start.10 = (f32[4,2,8,256]{3,2,1,0:T(8,128)S(1)}, f32[4,2,8,256]{3,2,1,0:T(8,128)S(1)}, u32[]{:S(2)}, u32[]{:S(2)}) collective-permute-start(f32[4,2,8,256]{3,2,1,0:T(8,128)S(1)} %collective-permute-done.8), channel_id=1, source_target_pairs={{0,4},{4,8},{8,12},{12,16},{16,20},{20,24},{24,28},{28,0},{1,5},{5... | collective-permute-start | bytes 196616 | tf_op jit(solution)/shard_map/ppermute | solution.py:171
